TPU v7x, 256 devices: a whole 4x4x8 slice. The times are simulated.
256 devices in a mesh: pipe: 2 (over core), dp: 4 (over x), fsdp: 32 (over z, y).
Axes of the slice: x: 4, y: 4, z: 8, core: 2. Of those that a mesh axis runs over, the one named last changes fastest.
Arguments:
- incoming: bfloat16 [1024, 6144], P(('pipe', 'dp'), 'fsdp'), may hold values from -6 to 6
- cotangent: bfloat16 [1024, 6144], P(('pipe', 'dp'), 'fsdp'), may hold values from -6 to 6
- weights: bfloat16 [2, 3, 6144, 16384], P('pipe', None, 'dp', 'fsdp'), may hold values from -0.078125 to 0.078125
- token_rows: int32 [1024], P(('pipe', 'dp')), may hold values from 0 to 127, as said below
- row_count: int32 [8], P(('pipe', 'dp')), may hold values from 1 to 128, as said below
- gate: float32 [1024], P(('pipe', 'dp')), may hold values from 0.1 to 1
Outputs:
- d_input: bfloat16 [1024, 6144], P(('pipe', 'dp'), 'fsdp')
- weight_grad: bfloat16 [2, 3, 6144, 16384], P('pipe', None, 'dp', 'fsdp')
Inputs may be any that keep to these rules, and one draw needn't show every extreme that they name: `token_rows`: in each group the 128 entries are a permutation of 0 to 127; the first row_count entries name the tokens routed to the expert. `row_count`: some group's count is 128 in every draw.
All inputs are finite; a program needn't handle non-finite values.
Results may differ from a plain program's by a relative error of at most 0.02.
Values may be sent and summed in bfloat16 or wider, within the bound.
A program may use at most 128 MiB of HBM per device.

v0:
```python
import jax
import jax.numpy as jnp
from jax import lax
from jax.sharding import PartitionSpec as P


def from_behind(block, axis, distance):
    devices = range(lax.axis_size(axis))
    route = [((i - distance) % len(devices), i) for i in devices]
    return lax.ppermute(block, axis, route)


def on_device(incoming, cotangent, weights, token_rows, row_count, gate):
    panel = weights[0]
    hidden_local = panel.shape[2]
    tok_count = cotangent.shape[0]
    shifted = from_behind(incoming, "pipe", 1)
    arrived, returned = (
        lax.all_gather(shifted, "fsdp", axis=1, tiled=True),
        lax.all_gather(cotangent, "fsdp", axis=1, tiled=True),
    )
    full_width = arrived.shape[1]
    gathered = lax.all_gather(panel, "dp", axis=1, tiled=True)
    w_in = gathered[0:2]
    w_down = gathered[2]
    routed = jnp.take(arrived, token_rows, axis=0)
    pre = jnp.einsum("td,kdh->kth", routed, w_in, preferred_element_type=jnp.float32)
    gate_pre = pre[0]
    up_pre = pre[1]
    sigmoid_gate = jax.nn.sigmoid(gate_pre)
    activated = (gate_pre * sigmoid_gate * up_pre).astype(jnp.bfloat16)
    live = lax.broadcasted_iota(jnp.int32, (tok_count, 1), 0) < row_count[0]
    row_gates = jnp.take(gate, token_rows)[:, None]
    weighted = row_gates * jnp.take(returned, token_rows, axis=0).astype(jnp.float32)
    scaled = jnp.where(live, weighted, 0.0).astype(jnp.bfloat16)
    d_act = jnp.dot(scaled, w_down, preferred_element_type=jnp.float32)
    d_gate = d_act * up_pre * sigmoid_gate * (1.0 + gate_pre * (1.0 - sigmoid_gate))
    d_up = d_act * gate_pre * sigmoid_gate
    d_pre = jnp.concatenate([d_gate, d_up], axis=1).astype(jnp.bfloat16)
    d_routed = lax.dot_general(
        d_pre.reshape(tok_count, 2, hidden_local),
        w_in,
        (((1, 2), (0, 2)), ((), ())),
        preferred_element_type=jnp.float32,
    )
    terms = jnp.zeros((tok_count, full_width), jnp.float32).at[token_rows].set(d_routed)
    d_input = lax.psum_scatter(terms.astype(jnp.bfloat16), "fsdp", scatter_dimension=1, tiled=True)
    routed_cols, scaled_cols = (
        lax.all_to_all(routed, "dp", split_axis=1, concat_axis=0, tiled=True),
        lax.all_to_all(scaled, "dp", split_axis=1, concat_axis=0, tiled=True),
    )
    d_pre_piece = lax.all_gather(d_pre, "dp", axis=0, tiled=True)
    act_piece = lax.all_gather(activated, "dp", axis=0, tiled=True)
    inner = (((0,), (0,)), ((), ()))
    grad_in = lax.dot_general(routed_cols, d_pre_piece, inner, preferred_element_type=jnp.float32)
    grad_down = lax.dot_general(scaled_cols, act_piece, inner, preferred_element_type=jnp.float32)
    local_grad = jnp.stack([grad_in[:, :hidden_local], grad_in[:, hidden_local:], grad_down])
    return (d_input, local_grad.astype(jnp.bfloat16)[None])


def solution(mesh):
    return jax.shard_map(
        on_device,
        mesh=mesh,
        in_specs=(
            P(("pipe", "dp"), "fsdp"),
            P(("pipe", "dp"), "fsdp"),
            P("pipe", None, "dp", "fsdp"),
            P(("pipe", "dp")),
            P(("pipe", "dp")),
            P(("pipe", "dp")),
        ),
        out_specs=(P(("pipe", "dp"), "fsdp"), P("pipe", None, "dp", "fsdp")),
        check_vma=False,
    )
```

profile of v0, /device:TPU:36, one launch (start us, length us, event | category | flops | bytes accessed | tf_op | source)
XLA Modules:
  0.0 612.3 jit_solution(17832061655891211123)
XLA Ops:
  7.2 0.7 all-gather.6.cloned.1.call-update
  8.1 1.4 collective-permute-done
  9.5 0.6 copy-done.4
  10.2 0.7 all-gather.12.cloned.1.call-update
  11.6 1.2 gather_fusion
  12.9 76.7 %all-gather.6.cloned.1.call-done = bf16[128,6144]{0,1:T(8,128)(2,1)} async-done(((bf16[128,192]{0,1:T(8,128)(2,1)}), bf16[128,6144]{0,1:T(8,128)(2,1)}) %all-gather.6.cloned.1.call-update) | async-done | bytes 1572880 | tf_op jit(solution)/shard_map/all_gather | solution.py:20
  89.6 1.7 copy.16
  91.3 1.5 gather_fusion.1
  92.8 0.7 select_convert_fusion
  93.5 73.9 %all-gather.8.cloned.1.call-done = bf16[128,6144]{0,1:T(8,128)(2,1)} async-done(((bf16[128,192]{0,1:T(8,128)(2,1)}), bf16[128,6144]{0,1:T(8,128)(2,1)}) %all-gather.8.cloned.1.call-update) | async-done | bytes 1572880 | tf_op jit(solution)/shard_map/all_gather | solution.py:19
  167.4 1.7 copy.17
  169.1 2.6 gather_fusion.2
  171.8 1.6 broadcast_select_fusion
  173.4 167.2 %all-gather.12.cloned.1.call-done = bf16[1,3,6144,512]{3,2,1,0:T(8,128)(2,1)} async-done(((bf16[1,3,1536,512]{3,2,1,0:T(8,128)(2,1)}), bf16[1,3,6144,512]{3,2,1,0:T(8,128)(2,1)}) %all-gather.12.cloned.1.call-update) | async-done | bytes 18874384 | tf_op jit(solution)/shard_map/all_gather | solution.py:23
  340.6 5.7 fusion.8
  346.3 3.9 multiply_convert_fusion.2
  350.2 0.8 pad_maximum_fusion.1
  351.0 1.3 copy.27
  352.3 5.5 all-to-all-start.1
  357.9 10.4 %fusion.2 = f32[128,6144]{1,0:T(8,128)} fusion(bf16[1,3,6144,512]{3,2,1,0:T(8,128)(2,1)} %all-gather.12.cloned.1.call-done, bf16[128,1,512]{2,0,1:T(8,128)(2,1)S(1)} %bitcast.73, bf16[128,1,512]{2,0,1:T(8,128)(2,1)S(1)} %bitcast.72), kind=kOutput, calls=%fused_computation.7 | convolution fusion | flops 1610743808 | bytes 15990784 | tf_op jit(solution)/shard_map/dot_general | solution.py:40
  368.2 4.4 scatter_custom_fusion
  372.7 1.3 convert_element_type.24
  374.0 2.6 copy.21
  376.6 1.4 copy-done.3
  378.0 1.3 copy.28
  379.3 4.9 all-to-all-done.1
  384.2 6.7 %all-to-all-start = ((bf16[128,4,1536]{2,0,1:T(8,128)(2,1)}), bf16[128,4,1536]{2,0,1:T(8,128)(2,1)S(1)}, u32[]{:S(2)}, u32[]{:S(2)}) async-start(bf16[128,4,1536]{2,0,1:T(8,128)(2,1)} %bitcast.65), calls=%async_computation | async-start | bytes 3145728 | tf_op jit(solution)/shard_map/all_to_all | solution.py:49
  390.9 26.2 %all_gather.19 = bf16[512,512]{1,0:T(8,128)(2,1)S(1)} all-gather(bf16[128,512]{1,0:T(8,128)(2,1)S(1)} %get-tuple-element.15), channel_id=1, replica_groups=mesh['pipe'=2,'dp'=4,'fsdp'=32] {'dp'}, dimensions={0}, use_global_device_ids=true | all-gather | bytes 655360 | tf_op jit(solution)/shard_map/all_gather | solution.py:53
  417.1 2.4 fusion.4
  419.6 3.1 convolution_convert_fusion
  422.9 2.5 pad_maximum_fusion
  425.4 180.4 %reduce-scatter.4.cloned.1.call-done = bf16[192,128]{1,0:T(8,128)(2,1)} async-done(((bf16[6144,128]{1,0:T(8,128)(2,1)}), bf16[192,128]{1,0:T(8,128)(2,1)}) %reduce-scatter.4.cloned.1.call-update) | async-done | bytes 49168
  (26 shorter events, 0.6 us)
Async XLA Ops:
  7.2 4.4 copy-start
  7.2 82.4 %all-gather.6.cloned.1.call-start = ((), (), s32[]{:S(2)}) async-start(), calls=%async_computation.3 | async-start | bytes 1622016 | tf_op jit(solution)/shard_map/all_gather | solution.py:20
  7.9 159.5 %all-gather.8.cloned.1.call-start = ((), (), s32[]{:S(2)}) async-start(), calls=%async_computation.4 | async-start | bytes 1622016 | tf_op jit(solution)/shard_map/all_gather | solution.py:19
  8.0 1.5 collective-permute-start
  9.5 0.6 copy-start.4
  10.1 1.4 copy-start.5
  10.1 330.4 %all-gather.12.cloned.1.call-start = ((), (), s32[]{:S(2)}) async-start(), calls=%async_computation.6 | async-start | bytes 23592960 | tf_op jit(solution)/shard_map/all_gather | solution.py:23
  10.9 408.7 %all-gather.10.cloned.1.call-start = ((), (), s32[]{:S(2)}) async-start(), calls=%async_computation.5 | async-start | bytes 1310720 | tf_op jit(solution)/shard_map/all_gather | solution.py:52
  173.4 172.9 %copy-start.2 = (bf16[128,6144]{1,0:T(8,128)(2,1)}, bf16[128,6144]{1,0:T(8,128)(2,1)S(1)}, u32[]{:S(2)}) copy-start(bf16[128,6144]{1,0:T(8,128)(2,1)S(1)} %broadcast_select_fusion) | copy-start | bytes 4718596
  352.3 31.9 %all-to-all-start.1 = ((bf16[128,4,1536]{2,0,1:T(8,128)(2,1)}), bf16[128,4,1536]{2,0,1:T(8,128)(2,1)}, u32[]{:S(2)}, u32[]{:S(2)}) async-start(bf16[128,4,1536]{2,0,1:T(8,128)(2,1)} %bitcast.64), calls=%async_computation.1 | async-start | bytes 3145728 | tf_op jit(solution)/shard_map/all_to_all | solution.py:50
  357.9 247.9 %reduce-scatter.4.cloned.1.call-start = ((), (), s32[]{:S(2)}) async-start(), calls=%async_computation.7 | async-start | bytes 1622016
  376.6 1.4 copy-start.3
  384.2 35.3 %all-to-all-start = ((bf16[128,4,1536]{2,0,1:T(8,128)(2,1)}), bf16[128,4,1536]{2,0,1:T(8,128)(2,1)S(1)}, u32[]{:S(2)}, u32[]{:S(2)}) async-start(bf16[128,4,1536]{2,0,1:T(8,128)(2,1)} %bitcast.65), calls=%async_computation | async-start | bytes 3145728 | tf_op jit(solution)/shard_map/all_to_all | solution.py:49
  422.9 182.9 %copy-start.1 = (f32[128]{0:T(128)S(1)}, f32[128]{0:T(128)}, u32[]{:S(2)}) copy-start(f32[128]{0:T(128)} %param.13) | copy-start | bytes 1540
Sparse Core Ops, SparseCore 0:
  10.6 78.9 all-gather.5
  92.7 74.6 all-gather.7
  169.2 171.2 all-gather.11
  351.1 33.5 all-gather.9
  389.0 216.7 reduce-scatter.3
where the time goes:
time: 614 us; the launch traced here: 612 us
  waiting for transfers between devices  506 us (82%)
  blocking collectives  26.2 us (4%)
  matrix products  25.5 us (4%)
  local copies, waits for them, and re-layouts  20.6 us (3%)
  between operations  14.6 us (2%)
  starting transfers between devices  12.5 us (2%)
  other arithmetic  6.93 us (1%)
    unnamed x6, waiting for transfers between devices  182 us
    all_gather x1, waiting for transfers between devices, on_device(): gathered = lax.all_gather(panel, 'dp', axis=1, tiled=True)  167 us
    all_gather x1, waiting for transfers between devices, on_device(): lax.all_gather(cotangent, 'fsdp', axis=1, tiled=True)  76.7 us
    all_gather x1, waiting for transfers between devices, on_device(): lax.all_gather(shifted, 'fsdp', axis=1, tiled=True)  73.9 us
    all_gather x1, blocking collectives, on_device(): act_piece = lax.all_gather(activated, 'dp', axis=0, tiled=True)  26.2 us
  transfers between devices with their start and end apart: 8, of which 6 were waited for; matrix products, arithmetic and copies ran while one was open for 7% of the time, Pallas kernels for 0%

commit v1 on v0

v1 whole, which is shorter than its diff:
```python
import functools

import jax
import jax.numpy as jnp
from jax import lax
from jax.experimental import pallas as pl
from jax.experimental.pallas import tpu as pltpu
from jax.sharding import PartitionSpec as P

NX, NY, NZ = 4, 4, 8
TOK = 128
COLS = 192
ROWS_D = 1536
HID = 512
CUT = 80
CHUNK = 48
F32 = jnp.float32
BF16 = jnp.bfloat16
MESH = pl.DeviceIdType.MESH
N_RECV = 160
N_SEND = 224


class Links:
    def __init__(self, send_sem, recv_sem, me):
        self.send_sem, self.recv_sem, self.me = send_sem, recv_sem, me
        self.recv_at, self.sent, self.n_sent = {}, [], 0

    def recv(self, key):
        at = self.recv_at.setdefault(key, len(self.recv_at))
        return self.recv_sem.at[at]

    def put(self, key, src, dst, to, is_self=None):
        send = self.send_sem.at[self.n_sent]
        self.n_sent += 1
        recv = self.recv(key)
        copy = pltpu.make_async_remote_copy(
            src_ref=src, dst_ref=dst, send_sem=send, recv_sem=recv,
            device_id=to, device_id_type=MESH)
        if is_self is None:
            copy.start()
        else:
            pl.when(jnp.logical_not(is_self))(copy.start)
            pl.when(is_self)(pltpu.make_async_copy(src, dst, recv).start)
        self.sent.append((copy, is_self))

    def take(self, key, dst):
        pltpu.make_async_remote_copy(
            src_ref=dst, dst_ref=dst, send_sem=self.send_sem.at[0], recv_sem=self.recv(key),
            device_id=self.me, device_id_type=MESH).wait_recv()

    def finish(self):
        for copy, is_self in self.sent:
            if is_self is None:
                copy.wait_send()
            else:
                pl.when(jnp.logical_not(is_self))(copy.wait_send)


def flip(block):
    return block.astype(F32).T


def kernel(inc_ref, cot_ref, w_hbm, rows_ref, count_ref, gate_ref, din_ref, wg_hbm,
           w, first, cols, flat, part, own, xin, d_all, share, yin, ysum, zin, zsum, fin, wg,
           send_sem, recv_sem, w_sem, wg_sem):
    p = lax.axis_index("pipe")
    x = lax.axis_index("dp")
    f = lax.axis_index("fsdp")
    z, y = lax.div(f, NY), lax.rem(f, NY)

    def dev(px, xx, yy, zz):
        return (px, xx, zz * NY + yy)

    def at_x(o):
        return lax.rem(x + o + NX, NX)

    def at_y(o):
        return lax.rem(y + o + NY, NY)

    def at_z(o):
        return lax.rem(z + o + NZ, NZ)

    def to_x(o):
        return dev(p, at_x(o), y, z)

    def to_y(o):
        return dev(p, x, at_y(o), z)

    def to_z(o):
        return dev(p, x, y, at_z(o))

    home_x, home_z = lax.div(z, 2), 2 * x + lax.rem(z, 2)
    relay = dev(1 - p, home_x, y, home_z)
    home = dev(p, home_x, y, home_z)
    home_self = jnp.logical_and(home_x == x, home_z == z)
    end_z = 2 * x + lax.div(z, NZ // 2)
    fin_self = end_z == z

    barrier = pltpu.get_barrier_semaphore()

    def greet(to):
        pl.semaphore_signal(barrier, inc=1, device_id=to, device_id_type=MESH)

    greet(relay)
    pl.when(jnp.logical_not(home_self))(lambda: greet(home))
    for o in range(1, NX):
        greet(to_x(o))
    for o in range(1, NY):
        greet(to_y(o))
    for o in range(1, NZ):
        greet(to_z(o))
    for j in range(4):
        to = dev(p, at_x(j), y, end_z)
        if j == 0:
            pl.when(jnp.logical_not(fin_self))(functools.partial(greet, to))
        else:
            greet(to)
        src_z = 4 * lax.rem(z, 2) + j
        same = jnp.logical_and(home_x == x, src_z == z)
        pl.when(jnp.logical_not(same))(functools.partial(greet, dev(p, home_x, y, src_z)))

    w_copies = [pltpu.make_async_copy(w_hbm.at[0, i], w.at[i], w_sem.at[i]) for i in range(3)]
    for copy in w_copies:
        copy.start()

    first[0, 0:128] = flip(inc_ref[:, 0:128]).astype(BF16)
    first[0, 128:192] = flip(inc_ref[:, 128:192]).astype(BF16)
    down = lax.broadcasted_iota(jnp.int32, (TOK, TOK), 0)
    across = lax.broadcasted_iota(jnp.int32, (TOK, TOK), 1)
    routed_here = jnp.logical_and(down == rows_ref[...], across < count_ref[...])
    live = jnp.sum(jnp.where(routed_here, 1.0, 0.0), axis=1, keepdims=True) > 0.5
    gate = jnp.sum(jnp.where(down == across, gate_ref[...], 0.0), axis=1, keepdims=True)
    scaled = jnp.where(live, gate * cot_ref[...].astype(F32), 0.0).astype(BF16)
    first[1, 0:128] = flip(scaled[:, 0:128]).astype(BF16)
    first[1, 128:192] = flip(scaled[:, 128:192]).astype(BF16)

    expected = 1 + (NX - 1) + (NY - 1) + (NZ - 1) + 8
    pl.semaphore_wait(barrier, expected + jnp.where(home_self, 0, 1) - jnp.where(fin_self, 2, 0))

    links = Links(send_sem, recv_sem, to_z(1))
    put, take = links.put, links.take

    put(("home", 0), first.at[0], cols.at[0, home_z, y], relay)
    put(("home", 1), first.at[1], cols.at[1, home_z, y], home, home_self)

    low = pl.ds(0, CUT)
    high = pl.ds(CUT, COLS - CUT)

    def gather_steps(a):
        buf = cols.at[a]

        def piece(j, o=0):
            return buf.at[at_z(j), at_y(o), high]

        def block(j, part_of=slice(None)):
            if part_of == slice(None):
                return buf.at[at_z(j), :, low]
            return buf.at[at_z(j), pl.ds(part_of.start, 2), low]

        def spread(j):
            put(("y", a, 3, j % NZ), piece(j), piece(j), to_y(1))
            put(("y", a, 1, j % NZ), piece(j), piece(j), to_y(-1))

        def hop(s):
            if s <= 4:
                put(("f", a, s), piece(1 - s), piece(1 - s), to_z(1))
            if s <= 3:
                put(("b", a, s), piece(s - 1), piece(s - 1), to_z(-1))

        def block_hop(s):
            if s <= 3:
                put(("bf", a, s), block(1 - s), block(1 - s), to_z(1))
                put(("bb", a, s), block(s - 1), block(s - 1), to_z(-1))
            else:
                put(("bf", a, s), block(1 - s, slice(0, 2)), block(1 - s, slice(0, 2)), to_z(1))
                put(("bb", a, s), block(s - 1, slice(2, 4)), block(s - 1, slice(2, 4)), to_z(-1))

        def forward_up(j):
            take(("y", a, 3, j % NZ), piece(j, -1))
            put(("y", a, 2, j % NZ), piece(j, -1), piece(j, -1), to_y(1))

        def forward_down(j):
            take(("y", a, 1, j % NZ), piece(j, 1))
            put(("y", a, 2, j % NZ), piece(j, 1), piece(j, 1), to_y(-1))

        def start():
            take(("home", a), buf.at[z, y])
            for o in (1, 3, 2):
                own_low = buf.at[z, y, low]
                put(("ly", a, (NY - o) % NY), own_low, own_low, to_y(o))
            hop(1)
            spread(0)

        def middle(s):
            take(("f", a, s), piece(-s))
            if s < 4:
                put(("f", a, s + 1), piece(-s), piece(-s), to_z(1))
            if s <= 3:
                take(("b", a, s), piece(s))
                if s < 3:
                    put(("b", a, s + 1), piece(s), piece(s), to_z(-1))
            if s == 1:
                for o in range(1, NY):
                    take(("ly", a, o), buf.at[z, at_y(o), low])
                block_hop(1)
            else:
                take(("bf", a, s - 1), block(1 - s))
                take(("bb", a, s - 1), block(s - 1))
                block_hop(s)
            spread(-s)
            if s <= 3:
                spread(s)
            if s >= 2:
                forward_up(1 - s)
            forward_down(s - 1)

        def close():
            forward_up(-4)
            take(("bf", a, 4), block(-4, slice(0, 2)))
            take(("bb", a, 4), block(4, slice(2, 4)))

        def drain():
            for j in range(-4, 4):
                if j >= 0:
                    take(("y", a, 3, j % NZ), piece(j, -1))
                else:
                    take(("y", a, 1, j % NZ), piece(j, 1))
                take(("y", a, 2, j % NZ), piece(j, 2))

        return [start] + [functools.partial(middle, s) for s in range(1, 5)] + [close, drain]

    def flatten(a):
        def one(g, _):
            turned = flip(cols[a, pl.ds(2 * g, 2)].reshape(ROWS_D, TOK)).astype(BF16)
            flat[pl.ds(pl.multiple_of(g * TOK, TOK), TOK), :] = turned
            return 0
        lax.fori_loop(0, NX, one, 0)

    def project(i):
        for t in range(2):
            span = slice(t * 256, t * 256 + 256)
            out = jnp.dot(flat[...], w[i, :, span], preferred_element_type=F32)
            part[:, i, :, span] = out.astype(BF16).reshape(NX, TOK, 256)

    def send_part(name, lo, n):
        for o in (2, 1, 3):
            put((name, NX - o), part.at[at_x(o), pl.ds(lo, n)], xin.at[NX - o - 1, pl.ds(lo, n)], to_x(o))

    def take_part(name, lo, n):
        for o in range(1, NX):
            take((name, o), xin.at[o - 1, pl.ds(lo, n)])

    def total(i):
        out = part[x, i].astype(F32)
        for o in range(1, NX):
            out = out + xin[o - 1, i].astype(F32)
        return out

    routed_steps, scaled_steps = gather_steps(0), gather_steps(1)
    routed_steps[0]()
    routed_steps[1]()
    for k in range(2, 7):
        scaled_steps[k - 2]()
        routed_steps[k]()
    for copy in w_copies:
        copy.wait()
    flatten(0)
    project(0)
    project(1)
    send_part("gu", 0, 2)
    scaled_steps[5]()
    scaled_steps[6]()
    flatten(1)
    project(2)
    send_part("d", 2, 1)

    take_part("gu", 0, 2)
    g_pre = total(0)
    u_pre = total(1)
    sigma = 1.0 / (1.0 + jnp.exp(-g_pre))
    silu = g_pre * sigma
    d_all[x, 2] = (silu * u_pre).astype(BF16)
    own[0] = u_pre * sigma * (1.0 + g_pre * (1.0 - sigma))
    own[1] = silu

    def send_rows(name, lo, n):
        for o in (2, 1, 3):
            mine = d_all.at[x, pl.ds(lo, n)]
            put((name, NX - o), mine, mine, to_x(o))

    take_part("d", 2, 1)
    d_act = total(2)
    d_all[x, 0] = (d_act * own[0]).astype(BF16)
    d_all[x, 1] = (d_act * own[1]).astype(BF16)
    send_rows("dgu", 0, 2)
    send_rows("act", 2, 1)

    nt = (((1,), (1,)), ((), ()))

    def make_share(n, g):
        for k in range(2):
            rows = slice(768 * k, 768 * k + 768)
            out = lax.dot_general(w[0, rows], d_all[g, 0], nt, preferred_element_type=F32)
            out = out + lax.dot_general(w[1, rows], d_all[g, 1], nt, preferred_element_type=F32)
            share[n, k] = out.astype(BF16).reshape(NY, COLS, TOK)
        for o in (2, 1, 3):
            put(("sy", n, NY - o), share.at[n, :, at_y(o)], yin.at[n, NY - o - 1], to_y(o))

    def reduce_y(n):
        out = share[n, :, y].astype(F32)
        for o in range(1, NY):
            take(("sy", n, o), yin.at[n, o - 1])
            out = out + yin[n, o - 1].astype(F32)
        ysum[n] = out.astype(BF16).reshape(NZ, CHUNK, TOK)
        for o in (4, 3, 5, 2, 6, 1, 7):
            put(("sz", n, NZ - o), ysum.at[n, at_z(o)], zin.at[n, NZ - o - 1], to_z(o))

    def reduce_z(n, o_x):
        out = ysum[n, z].astype(F32)
        for o in range(1, NZ):
            take(("sz", n, o), zin.at[n, o - 1])
            out = out + zin[n, o - 1].astype(F32)
        zsum[n] = out.astype(BF16)
        put(("end",), zsum.at[n], fin.at[lax.rem(z, 4)], dev(p, at_x(o_x), y, end_z),
            fin_self if o_x == 0 else None)

    def weight_grad(i):
        a = 0 if i < 2 else 1
        right = d_all[:, i].reshape(NX * TOK, HID)
        for k in range(2):
            for q in range(2):
                left = jnp.concatenate(
                    [cols[a, 2 * g + k, pl.ds(2 * q, 2)].reshape(384, TOK) for g in range(NX)], axis=1)
                out = jnp.dot(left, right, preferred_element_type=F32)
                wg[i, 768 * k + 384 * q:768 * k + 384 * q + 384] = out.astype(BF16)
        pltpu.make_async_copy(wg.at[i], wg_hbm.at[0, i], wg_sem.at[i]).start()

    order = (0, 1, 3, 2)
    for n, o in enumerate(order):
        if o:
            take(("dgu", o), d_all.at[at_x(o), pl.ds(0, 2)])
        make_share(n, at_x(o))
        if n >= 1:
            reduce_y(n - 1)
        if n >= 2:
            reduce_z(n - 2, order[n - 2])
    weight_grad(0)
    reduce_y(3)
    reduce_z(2, order[2])
    weight_grad(1)
    reduce_z(3, order[3])
    for o in range(1, NX):
        take(("act", o), d_all.at[at_x(o), pl.ds(2, 1)])
    weight_grad(2)
    take(("end",), fin)
    done = fin[...].reshape(COLS, TOK)
    din_ref[:, 0:128] = flip(done[0:128]).astype(BF16)
    din_ref[:, 128:192] = flip(done[128:192]).astype(BF16)
    links.finish()
    for i in range(3):
        pltpu.make_async_copy(wg.at[i], wg_hbm.at[0, i], wg_sem.at[i]).wait()
    assert len(links.recv_at) <= N_RECV and links.n_sent <= N_SEND


def on_device(incoming, cotangent, weights, token_rows, row_count, gate):
    vmem = pl.BlockSpec(memory_space=pltpu.VMEM)
    anywhere = pl.BlockSpec(memory_space=pl.ANY)
    return pl.pallas_call(
        kernel,
        out_shape=(jax.ShapeDtypeStruct((TOK, COLS), BF16),
                   jax.ShapeDtypeStruct((1, 3, ROWS_D, HID), BF16)),
        in_specs=[vmem, vmem, anywhere, vmem, vmem, vmem],
        out_specs=(vmem, anywhere),
        scratch_shapes=[
            pltpu.VMEM((3, ROWS_D, HID), BF16),
            pltpu.VMEM((2, COLS, TOK), BF16),
            pltpu.VMEM((2, NZ, NY, COLS, TOK), BF16),
            pltpu.VMEM((NX * TOK, ROWS_D), BF16),
            pltpu.VMEM((NX, 3, TOK, HID), BF16),
            pltpu.VMEM((2, TOK, HID), F32),
            pltpu.VMEM((NX - 1, 3, TOK, HID), BF16),
            pltpu.VMEM((NX, 3, TOK, HID), BF16),
            pltpu.VMEM((NX, 2, NY, COLS, TOK), BF16),
            pltpu.VMEM((NX, NY - 1, 2, COLS, TOK), BF16),
            pltpu.VMEM((NX, NZ, CHUNK, TOK), BF16),
            pltpu.VMEM((NX, NZ - 1, CHUNK, TOK), BF16),
            pltpu.VMEM((NX, CHUNK, TOK), BF16),
            pltpu.VMEM((NX, CHUNK, TOK), BF16),
            pltpu.VMEM((3, ROWS_D, HID), BF16),
            pltpu.SemaphoreType.DMA((N_SEND,)),
            pltpu.SemaphoreType.DMA((N_RECV,)),
            pltpu.SemaphoreType.DMA((3,)),
            pltpu.SemaphoreType.DMA((3,)),
        ],
        compiler_params=pltpu.CompilerParams(
            collective_id=0, has_side_effects=True, vmem_limit_bytes=50 << 20),
        cost_estimate=pl.CostEstimate(flops=6_400_000_000, bytes_accessed=10_000_000, transcendentals=65536),
        name="expert",
    )(incoming, cotangent, weights, token_rows.reshape(1, TOK), row_count.reshape(1, 1), gate.reshape(1, TOK))


def solution(mesh):
    return jax.shard_map(
        on_device,
        mesh=mesh,
        in_specs=(
            P(("pipe", "dp"), "fsdp"),
            P(("pipe", "dp"), "fsdp"),
            P("pipe", None, "dp", "fsdp"),
            P(("pipe", "dp")),
            P(("pipe", "dp")),
            P(("pipe", "dp")),
        ),
        out_specs=(P(("pipe", "dp"), "fsdp"), P("pipe", None, "dp", "fsdp")),
        check_vma=False,
    )
```

time: 614 us -> 113 us (0.18)
  waiting for transfers between devices: 506 us -> 0 us
  Pallas kernels: 0 us -> 103 us
  blocking collectives: 26.2 us -> 0 us
  matrix products: 25.5 us -> 0 us
  between operations: 14.6 us -> 1.31 us
  starting transfers between devices: 12.5 us -> 0 us
  local copies, waits for them, and re-layouts: 20.6 us -> 8.65 us
  other arithmetic: 6.93 us -> 0 us
    all_gather x4 -> x0, waiting for transfers between devices: 318 us -> none  [the longest x1 167 us: on_device(): gathered = lax.all_gather(panel, 'dp', axis=1, tiled=True)]
    unnamed x6 -> x0, waiting for transfers between devices: 182 us -> none
    pallas_call x0 -> x1, Pallas kernels: none -> 103 us  [on_device(): pl.pallas_call(kernel, out_shape=(jax.ShapeDtypeStruct((TOK, COLS), BF16)...]
    all_gather x1 -> x0, blocking collectives: 26.2 us -> none  [on_device(): act_piece = lax.all_gather(activated, 'dp', axis=0, tiled=True)]
    dot_general x5 -> x0, matrix products: 25.5 us -> none  [the longest x1 10.4 us: on_device(): lax.dot_general(d_pre.reshape(tok_count, 2, hidden_local), w_in, (((1, 2)...]
    all_to_all x2 -> x0, starting transfers between devices: 12.3 us -> none  [the longest x1 6.71 us: on_device(): lax.all_to_all(routed, 'dp', split_axis=1, concat_axis=0, tiled=True)]
  transfers between devices with their start and end apart: 8 -> 0, of which waited for: 6 -> 0; matrix products, arithmetic and copies ran while one was open for 7% -> 0% of each run, Pallas kernels for 0% -> 0%
where the time goes in v1:
time: 113 us
  Pallas kernels  103 us (91%)
  local copies, waits for them, and re-layouts  8.65 us (8%)
  between operations  1.31 us (1%)
    pallas_call x1, Pallas kernels, on_device(): pl.pallas_call(kernel, out_shape=(jax.ShapeDtypeStruct((TOK, COLS), BF16)...  103 us
    unnamed x7, local copies, waits for them, and re-layouts  7.92 us

profile of v1, /device:TPU:36, one launch (start us, length us, event | category | flops | bytes accessed | tf_op | source)
XLA Modules:
  0.0 112.8 jit_solution(11431297079365066941)
XLA Ops:
  1.3 0.9 copy.8.inc_ref
  2.2 0.9 copy.9.cot_ref
  3.1 0.0 copy-start
  3.1 0.6 copy-done
  3.7 0.0 copy-start.1
  3.7 0.7 copy-done.1
  4.4 102.9 %expert.1 = (bf16[128,192]{1,0:T(8,128)(2,1)S(1)}, bf16[1,3,1536,512]{3,2,1,0:T(8,128)(2,1)}) custom-call(bf16[128,192]{1,0:T(8,128)(2,1)S(1)} %copy.8.inc_ref, bf16[128,192]{1,0:T(8,128)(2,1)S(1)} %copy.9.cot_ref, bf16[1,3,1536,512]{3,2,1,0:T(8,128)(2,1)} %w_hbm.1, s32[1,128]{1,0:T(1,128)S(1)} %bitcast.4, s32[1,1]{1,0:T(1,128)} %bitcast.3.count_ref, ...), custom_call_target="tpu_custom_call" | custom-call | flops 6400000000 | bytes 10000000 | tf_op jit(solution)/shard_map/expert/pallas_call | solution.py:369
  107.3 0.7 copy.10
  108.0 4.8 %copy.13 = bf16[1,3,1536,512]{3,2,1,0:T(8,128)(2,1)} copy(bf16[1,3,1536,512]{3,2,1,0:T(8,128)(2,1)} %get-tuple-element.7) | data formatting | bytes 9437184
Async XLA Ops:
  3.1 0.7 copy-start
  3.7 0.7 copy-start.1

commit v2 on v1

v2 whole, which is shorter than its diff:
```python
import functools

import jax
import jax.numpy as jnp
from jax import lax
from jax.experimental import pallas as pl
from jax.experimental.pallas import tpu as pltpu
from jax.sharding import PartitionSpec as P

NX, NY, NZ = 4, 4, 8
TOK = 128
COLS = 192
ROWS_D = 1536
HID = 512
CUT = 80
CHUNK = 48
F32 = jnp.float32
BF16 = jnp.bfloat16
MESH = pl.DeviceIdType.MESH
N_RECV = 256
N_SEND = 288


class Links:
    def __init__(self, send_sem, recv_sem, me):
        self.send_sem, self.recv_sem, self.me = send_sem, recv_sem, me
        self.recv_at, self.sent, self.n_sent = {}, [], 0

    def recv(self, key):
        at = self.recv_at.setdefault(key, len(self.recv_at))
        return self.recv_sem.at[at]

    def put(self, key, src, dst, to, is_self=None):
        send = self.send_sem.at[self.n_sent]
        self.n_sent += 1
        recv = self.recv(key)
        copy = pltpu.make_async_remote_copy(
            src_ref=src, dst_ref=dst, send_sem=send, recv_sem=recv,
            device_id=to, device_id_type=MESH)
        if is_self is None:
            copy.start()
        else:
            pl.when(jnp.logical_not(is_self))(copy.start)
            pl.when(is_self)(pltpu.make_async_copy(src, dst, recv).start)
        self.sent.append((copy, is_self))

    def take(self, key, dst):
        pltpu.make_async_remote_copy(
            src_ref=dst, dst_ref=dst, send_sem=self.send_sem.at[0], recv_sem=self.recv(key),
            device_id=self.me, device_id_type=MESH).wait_recv()

    def finish(self):
        for copy, is_self in self.sent:
            if is_self is None:
                copy.wait_send()
            else:
                pl.when(jnp.logical_not(is_self))(copy.wait_send)


def flip(block):
    return block.astype(F32).T


def kernel(inc_hbm, cot_hbm, w_hbm, rows_hbm, count_ref, gate_hbm, din_ref, wg,
           w, first, rows_ref, gate_ref, cols, flat, part, own, via, xin, d_all, share, yin, ysum, zin, zsum, fin,
           send_sem, recv_sem, w_sem):
    p = lax.axis_index("pipe")
    x = lax.axis_index("dp")
    f = lax.axis_index("fsdp")
    z, y = lax.div(f, NY), lax.rem(f, NY)

    def dev(px, xx, yy, zz):
        return (px, xx, zz * NY + yy)

    def at_x(o):
        return lax.rem(x + o + NX, NX)

    def at_y(o):
        return lax.rem(y + o + NY, NY)

    def at_z(o):
        return lax.rem(z + o + NZ, NZ)

    def to_x(o):
        return dev(p, at_x(o), y, z)

    def to_y(o):
        return dev(p, x, at_y(o), z)

    def to_z(o):
        return dev(p, x, y, at_z(o))

    home_x, home_z = lax.div(z, 2), 2 * x + lax.rem(z, 2)
    relay = dev(1 - p, home_x, y, home_z)
    home = dev(p, home_x, y, home_z)
    home_self = jnp.logical_and(home_x == x, home_z == z)
    end_z = 2 * x + lax.div(z, NZ // 2)
    fin_self = end_z == z

    barrier = pltpu.get_barrier_semaphore()

    def greet(to):
        pl.semaphore_signal(barrier, inc=1, device_id=to, device_id_type=MESH)

    greet(relay)
    pl.when(jnp.logical_not(home_self))(lambda: greet(home))
    for o in range(1, NX):
        greet(to_x(o))
    for o in range(1, NY):
        greet(to_y(o))
    for o in range(1, NZ):
        greet(to_z(o))
    for j in range(4):
        to = dev(p, at_x(j), y, end_z)
        if j == 0:
            pl.when(jnp.logical_not(fin_self))(functools.partial(greet, to))
        else:
            greet(to)
        src_z = 4 * lax.rem(z, 2) + j
        same = jnp.logical_and(home_x == x, src_z == z)
        pl.when(jnp.logical_not(same))(functools.partial(greet, dev(p, home_x, y, src_z)))

    small = [pltpu.make_async_copy(cot_hbm, first.at[0], w_sem.at[3]),
             pltpu.make_async_copy(rows_hbm, rows_ref, w_sem.at[4]),
             pltpu.make_async_copy(gate_hbm, gate_ref, w_sem.at[5])]
    w_copies = [pltpu.make_async_copy(w_hbm.at[0, i], w.at[i], w_sem.at[i]) for i in range(3)]
    for copy in small + w_copies:
        copy.start()
    for copy in small:
        copy.wait()

    down = lax.broadcasted_iota(jnp.int32, (TOK, TOK), 0)
    across = lax.broadcasted_iota(jnp.int32, (TOK, TOK), 1)
    named = jnp.sum(jnp.where(down == across, rows_ref[...], 0).astype(F32), axis=1, keepdims=True)
    routed_here = jnp.logical_and(named == across.astype(F32), down < count_ref[...])
    live = jnp.sum(jnp.where(routed_here, 1.0, 0.0), axis=0, keepdims=True) > 0.5
    first[1] = jnp.where(live, gate_ref[...] * first[0].astype(F32), 0.0).astype(BF16)

    expected = 1 + (NX - 1) + (NY - 1) + (NZ - 1) + 8
    pl.semaphore_wait(barrier, expected + jnp.where(home_self, 0, 1) - jnp.where(fin_self, 2, 0))

    links = Links(send_sem, recv_sem, to_z(1))
    put, take = links.put, links.take

    put(("home", 0), inc_hbm, cols.at[0, home_z, y], relay)

    low = pl.ds(0, CUT)
    high = pl.ds(CUT, COLS - CUT)

    def gather_steps(a):
        buf = cols.at[a]

        def piece(j, o=0):
            return buf.at[at_z(j), at_y(o), high]

        def block(j, o):
            return buf.at[at_z(j), at_y(o), low]

        def spread(j):
            put(("y", a, 3, j % NZ), piece(j), piece(j), to_y(1))
            put(("y", a, 1, j % NZ), piece(j), piece(j), to_y(-1))

        def block_hop(s, o):
            if s <= 3 or o < 2:
                put(("bf", a, s, o), block(1 - s, o), block(1 - s, o), to_z(1))
            if s <= 3 or o >= 2:
                put(("bb", a, s, o), block(s - 1, o), block(s - 1, o), to_z(-1))

        def forward_up(j):
            take(("y", a, 3, j % NZ), piece(j, -1))
            put(("y", a, 2, j % NZ), piece(j, -1), piece(j, -1), to_y(1))

        def forward_down(j):
            take(("y", a, 1, j % NZ), piece(j, 1))
            put(("y", a, 2, j % NZ), piece(j, 1), piece(j, 1), to_y(-1))

        def start():
            take(("home", a), buf.at[z, y])
            for o in (1, 3, 2):
                put(("ly", a, NY - o), block(0, 0), block(0, 0), to_y(o))
            put(("f", a, 1), piece(0), piece(0), to_z(1))
            put(("b", a, 1), piece(0), piece(0), to_z(-1))
            block_hop(1, 0)
            spread(0)

        def middle(s):
            take(("f", a, s), piece(-s))
            if s < 4:
                put(("f", a, s + 1), piece(-s), piece(-s), to_z(1))
            if s <= 3:
                take(("b", a, s), piece(s))
                if s < 3:
                    put(("b", a, s + 1), piece(s), piece(s), to_z(-1))
            for o in (0, 1, 3, 2):
                if s == 1:
                    if o:
                        take(("ly", a, o), block(0, o))
                        block_hop(1, o)
                else:
                    take(("bf", a, s - 1, o), block(1 - s, o))
                    take(("bb", a, s - 1, o), block(s - 1, o))
                    block_hop(s, o)
            spread(-s)
            if s <= 3:
                spread(s)
            if s >= 2:
                forward_up(1 - s)
            forward_down(s - 1)

        def close():
            forward_up(-4)
            for o in range(NY):
                take(("bf" if o < 2 else "bb", a, 4, o), block(4, o))

        def drain():
            for j in (0, -1, 1, -2, 2, -3, 3, -4):
                if j >= 0:
                    take(("y", a, 3, j % NZ), piece(j, -1))
                else:
                    take(("y", a, 1, j % NZ), piece(j, 1))
                take(("y", a, 2, j % NZ), piece(j, 2))
                flatten(a, at_z(j))

        return [start] + [functools.partial(middle, s) for s in range(1, 5)] + [close, drain]

    def flatten(a, slot):
        turned = flip(cols[a, slot].reshape(NY * COLS, TOK)).astype(BF16)
        flat[lax.rem(slot, 2), pl.ds(pl.multiple_of(lax.div(slot, 2) * TOK, TOK), TOK), :] = turned

    def project(i):
        for t in range(2):
            span = slice(t * 256, t * 256 + 256)
            out = jnp.dot(flat[0], w[i, 0:768, span], preferred_element_type=F32)
            out = out + jnp.dot(flat[1], w[i, 768:1536, span], preferred_element_type=F32)
            part[:, i, :, span] = out.astype(BF16).reshape(NX, TOK, 256)

    upper, lower = pl.ds(0, TOK // 2), pl.ds(TOK // 2, TOK // 2)

    def part_out(i):
        put(("via", i, 3), part.at[at_x(2), i, upper], via.at[0, i], to_x(1))
        put(("via", i, 1), part.at[at_x(2), i, lower], via.at[1, i], to_x(-1))
        put(("part", i, 3, 1), part.at[at_x(1), i, lower], xin.at[0, i, lower], to_x(1))
        put(("part", i, 1, 0), part.at[at_x(-1), i, upper], xin.at[1, i, upper], to_x(-1))

    def part_on(i):
        take(("via", i, 3), via.at[0, i])
        right = part[at_x(1), i, 0:64].astype(F32) + via[0, i].astype(F32)
        part[at_x(1), i, 0:64] = right.astype(BF16)
        put(("part", i, 3, 0), part.at[at_x(1), i, upper], xin.at[0, i, upper], to_x(1))
        take(("via", i, 1), via.at[1, i])
        left = part[at_x(-1), i, 64:128].astype(F32) + via[1, i].astype(F32)
        part[at_x(-1), i, 64:128] = left.astype(BF16)
        put(("part", i, 1, 1), part.at[at_x(-1), i, lower], xin.at[1, i, lower], to_x(-1))

    def total(i):
        take(("part", i, 3, 1), xin.at[0, i, lower])
        take(("part", i, 1, 0), xin.at[1, i, upper])
        take(("part", i, 3, 0), xin.at[0, i, upper])
        take(("part", i, 1, 1), xin.at[1, i, lower])
        return part[x, i].astype(F32) + xin[0, i].astype(F32) + xin[1, i].astype(F32)

    def rows_out(i):
        mine = d_all.at[x, i]
        put(("row", i, 3), mine, mine, to_x(1))
        put(("row", i, 1), mine, mine, to_x(-1))

    def rows_on(i):
        take(("row", i, 3), d_all.at[at_x(-1), i])
        onward = d_all.at[at_x(-1), i, upper]
        put(("far", i, 0), onward, onward, to_x(1))
        take(("row", i, 1), d_all.at[at_x(1), i])
        onward = d_all.at[at_x(1), i, lower]
        put(("far", i, 1), onward, onward, to_x(-1))

    def rows_far(i):
        take(("far", i, 0), d_all.at[at_x(2), i, upper])
        take(("far", i, 1), d_all.at[at_x(2), i, lower])

    routed_steps, scaled_steps = gather_steps(0), gather_steps(1)
    routed_steps[0]()
    put(("home", 1), first.at[1], cols.at[1, home_z, y], home, home_self)
    routed_steps[1]()
    routed_steps[2]()
    for k in range(3, 6):
        scaled_steps[k - 3]()
        routed_steps[k]()
    for copy in w_copies:
        copy.wait()
    routed_steps[6]()
    project(0)
    part_out(0)
    scaled_steps[3]()
    project(1)
    part_out(1)
    scaled_steps[4]()
    part_on(0)
    scaled_steps[5]()
    part_on(1)
    scaled_steps[6]()
    project(2)
    part_out(2)

    g_pre = total(0)
    u_pre = total(1)
    sigma = 1.0 / (1.0 + jnp.exp(-g_pre))
    silu = g_pre * sigma
    d_all[x, 2] = (silu * u_pre).astype(BF16)
    own[0] = u_pre * sigma * (1.0 + g_pre * (1.0 - sigma))
    own[1] = silu
    part_on(2)
    d_act = total(2)
    d_all[x, 0] = (d_act * own[0]).astype(BF16)
    rows_out(0)
    d_all[x, 1] = (d_act * own[1]).astype(BF16)
    rows_out(1)
    rows_out(2)

    nt = (((1,), (1,)), ((), ()))

    def make_share(n, g):
        for k in range(2):
            rows = slice(768 * k, 768 * k + 768)
            out = lax.dot_general(w[0, rows], d_all[g, 0], nt, preferred_element_type=F32)
            out = out + lax.dot_general(w[1, rows], d_all[g, 1], nt, preferred_element_type=F32)
            share[n, k] = out.astype(BF16).reshape(NY, COLS, TOK)
        for o in (2, 1, 3):
            put(("sy", n, NY - o), share.at[n, :, at_y(o)], yin.at[n, NY - o - 1], to_y(o))

    def reduce_y(n):
        out = share[n, :, y].astype(F32)
        for o in range(1, NY):
            take(("sy", n, o), yin.at[n, o - 1])
            out = out + yin[n, o - 1].astype(F32)
        ysum[n] = out.astype(BF16).reshape(NZ, CHUNK, TOK)
        for o in (4, 3, 5, 2, 6, 1, 7):
            put(("sz", n, NZ - o), ysum.at[n, at_z(o)], zin.at[n, NZ - o - 1], to_z(o))

    def reduce_z(n, o_x):
        out = ysum[n, z].astype(F32)
        for o in range(1, NZ):
            take(("sz", n, o), zin.at[n, o - 1])
            out = out + zin[n, o - 1].astype(F32)
        zsum[n] = out.astype(BF16)
        put(("end",), zsum.at[n], fin.at[lax.rem(z, 4)], dev(p, at_x(o_x), y, end_z),
            fin_self if o_x == 0 else None)

    def weight_grad(i):
        a = 0 if i < 2 else 1
        right = d_all[:, i].reshape(NX * TOK, HID)
        for k in range(2):
            for q in range(2):
                left = jnp.concatenate(
                    [cols[a, 2 * g + k, pl.ds(2 * q, 2)].reshape(384, TOK) for g in range(NX)], axis=1)
                out = jnp.dot(left, right, preferred_element_type=F32)
                wg[0, i, 768 * k + 384 * q:768 * k + 384 * q + 384] = out.astype(BF16)

    order = (0, 1, 3, 2)
    make_share(0, x)
    rows_on(0)
    rows_on(1)
    make_share(1, at_x(1))
    reduce_y(0)
    make_share(2, at_x(-1))
    reduce_y(1)
    reduce_z(0, order[0])
    rows_on(2)
    rows_far(0)
    rows_far(1)
    make_share(3, at_x(2))
    reduce_y(2)
    reduce_z(1, order[1])
    weight_grad(0)
    reduce_y(3)
    reduce_z(2, order[2])
    weight_grad(1)
    reduce_z(3, order[3])
    rows_far(2)
    weight_grad(2)
    take(("end",), fin)
    din_ref[...] = fin[...].reshape(COLS, TOK)
    links.finish()
    assert len(links.recv_at) <= N_RECV and links.n_sent <= N_SEND


def in_hbm(array):
    return pltpu.with_memory_space_constraint(array, pltpu.HBM)


def on_device(incoming, cotangent, weights, token_rows, row_count, gate):
    vmem = pl.BlockSpec(memory_space=pltpu.VMEM)
    hbm = pl.BlockSpec(memory_space=pltpu.HBM)
    d_input, weight_grad = pl.pallas_call(
        kernel,
        out_shape=(jax.ShapeDtypeStruct((COLS, TOK), BF16),
                   jax.ShapeDtypeStruct((1, 3, ROWS_D, HID), BF16)),
        in_specs=[hbm, hbm, hbm, hbm, vmem, hbm],
        out_specs=(vmem, vmem),
        scratch_shapes=[
            pltpu.VMEM((3, ROWS_D, HID), BF16),
            pltpu.VMEM((2, COLS, TOK), BF16),
            pltpu.VMEM((1, TOK), jnp.int32),
            pltpu.VMEM((1, TOK), F32),
            pltpu.VMEM((2, NZ, NY, COLS, TOK), BF16),
            pltpu.VMEM((2, NX * TOK, ROWS_D // 2), BF16),
            pltpu.VMEM((NX, 3, TOK, HID), BF16),
            pltpu.VMEM((2, TOK, HID), F32),
            pltpu.VMEM((2, 3, TOK // 2, HID), BF16),
            pltpu.VMEM((2, 3, TOK, HID), BF16),
            pltpu.VMEM((NX, 3, TOK, HID), BF16),
            pltpu.VMEM((NX, 2, NY, COLS, TOK), BF16),
            pltpu.VMEM((NX, NY - 1, 2, COLS, TOK), BF16),
            pltpu.VMEM((NX, NZ, CHUNK, TOK), BF16),
            pltpu.VMEM((NX, NZ - 1, CHUNK, TOK), BF16),
            pltpu.VMEM((NX, CHUNK, TOK), BF16),
            pltpu.VMEM((NX, CHUNK, TOK), BF16),
            pltpu.SemaphoreType.DMA((N_SEND,)),
            pltpu.SemaphoreType.DMA((N_RECV,)),
            pltpu.SemaphoreType.DMA((6,)),
        ],
        compiler_params=pltpu.CompilerParams(
            collective_id=0, has_side_effects=True, vmem_limit_bytes=36 << 20),
        cost_estimate=pl.CostEstimate(flops=6_400_000_000, bytes_accessed=10_000_000, transcendentals=65536),
        name="expert",
    )(in_hbm(incoming.T), in_hbm(cotangent.T), in_hbm(weights), in_hbm(token_rows.reshape(1, TOK)),
      row_count.reshape(1, 1), in_hbm(gate.reshape(1, TOK)))
    return d_input.T, weight_grad


def solution(mesh):
    return jax.shard_map(
        on_device,
        mesh=mesh,
        in_specs=(
            P(("pipe", "dp"), "fsdp"),
            P(("pipe", "dp"), "fsdp"),
            P("pipe", None, "dp", "fsdp"),
            P(("pipe", "dp")),
            P(("pipe", "dp")),
            P(("pipe", "dp")),
        ),
        out_specs=(P(("pipe", "dp"), "fsdp"), P("pipe", None, "dp", "fsdp")),
        check_vma=False,
    )
```

time: 113 us -> 97.3 us (0.86)
  Pallas kernels: 103 us -> 93 us
  local copies, waits for them, and re-layouts: 8.65 us -> 2.81 us
    pallas_call x1, Pallas kernels: 103 us -> 93 us  [on_device(): pl.pallas_call(kernel, out_shape=(jax.ShapeDtypeStruct((COLS, TOK), BF16)...]
    unnamed x7 -> x2, local copies, waits for them, and re-layouts: 7.92 us -> 2.81 us
where the time goes in v2:
time: 97.3 us; the launch traced here: 97.1 us
  Pallas kernels  93 us (96%)
  local copies, waits for them, and re-layouts  2.81 us (3%)
  between operations  1.29 us (1%)
    pallas_call x1, Pallas kernels, on_device(): pl.pallas_call(kernel, out_shape=(jax.ShapeDtypeStruct((COLS, TOK), BF16)...  93 us
    unnamed x2, local copies, waits for them, and re-layouts  2.81 us

profile of v2, /device:TPU:36, one launch (start us, length us, event | category | flops | bytes accessed | tf_op | source)
XLA Modules:
  0.0 97.1 jit_solution(15747532941159431136)
XLA Ops:
  1.3 93.0 %expert.1 = (bf16[192,128]{1,0:T(8,128)(2,1)S(1)}, bf16[1,3,1536,512]{3,2,1,0:T(8,128)(2,1)S(1)}) custom-call(bf16[192,128]{1,0:T(8,128)(2,1)} %bitcast.8, bf16[192,128]{1,0:T(8,128)(2,1)} %bitcast.9, bf16[1,3,1536,512]{3,2,1,0:T(8,128)(2,1)} %w_hbm.1, s32[1,128]{1,0:T(1,128)} %bitcast.10, s32[1,1]{1,0:T(1,128)} %bitcast.6.count_ref, f32[1,128]{1,0:T(1,128)} %bitcast.11), custom_call_target="tpu_custom_call" | custom-call | flops 6400000000 | bytes 10000000 | tf_op jit(solution)/shard_map/expert/pallas_call | solution.py:392
  94.2 0.6 copy.11
  94.9 2.2 %copy.12 = bf16[1,3,1536,512]{3,2,1,0:T(8,128)(2,1)} copy(bf16[1,3,1536,512]{3,2,1,0:T(8,128)(2,1)S(1)} %get-tuple-element.9) | data formatting | bytes 9437184

commit v3 on v2

--- a/solution.py
+++ b/solution.py
@@ -90,20 +90,38 @@
     def to_z(o):
         return dev(p, x, y, at_z(o))
 
-    home_x, home_z = lax.div(z, 2), 2 * x + lax.rem(z, 2)
+    def slot_of(plane, m, k):
+        return lax.rem(2 * plane + NZ + (1 + m if k else -m), NZ)
+
+    def slot_holds(plane, slot):
+        back = lax.rem(2 * plane + NZ - slot, NZ)
+        k = (back > 3).astype(jnp.int32)
+        m = jnp.where(back > 3, NZ - 1 - back, back)
+        return lax.rem(plane + m, NX), k
+
+    home_x = lax.div(z, 2)
+    away = lax.rem(x - home_x + NX, NX)
+    home_z = jnp.where(lax.rem(z, 2) == 1, lax.rem(z + away, NZ), lax.rem(z - away + NZ, NZ))
+    from_x, from_k = slot_holds(x, z)
+    from_z = 2 * x + from_k
+    home_self = home_x == x
+    end_z = 2 * x + lax.div(z, NZ // 2)
+    fin_self = end_z == z
+
+    barrier = pltpu.get_barrier_semaphore()
+
+    def greet(to):
+        pl.semaphore_signal(barrier, inc=1, device_id=to, device_id_type=MESH)
+
     relay = dev(1 - p, home_x, y, home_z)
     home = dev(p, home_x, y, home_z)
-    home_self = jnp.logical_and(home_x == x, home_z == z)
-    end_z = 2 * x + lax.div(z, NZ // 2)
-    fin_self = end_z == z
-
-    barrier = pltpu.get_barrier_semaphore()
-
-    def greet(to):
-        pl.semaphore_signal(barrier, inc=1, device_id=to, device_id_type=MESH)
-
     greet(relay)
-    pl.when(jnp.logical_not(home_self))(lambda: greet(home))
+    greet(dev(1 - p, from_x, y, from_z))
+
+    @pl.when(jnp.logical_not(home_self))
+    def _():
+        greet(home)
+        greet(dev(p, from_x, y, from_z))
     for o in range(1, NX):
         greet(to_x(o))
     for o in range(1, NY):
@@ -126,6 +144,14 @@
     w_copies = [pltpu.make_async_copy(w_hbm.at[0, i], w.at[i], w_sem.at[i]) for i in range(3)]
     for copy in small + w_copies:
         copy.start()
+    expected = 2 + (NX - 1) + (NY - 1) + (NZ - 1) + 8
+    pl.semaphore_wait(barrier, expected + jnp.where(home_self, 0, 2) - jnp.where(fin_self, 2, 0))
+
+    links = Links(send_sem, recv_sem, to_z(1))
+    put, take = links.put, links.take
+
+    put(("home", 0), inc_hbm, cols.at[0, home_z, y], relay)
+
     for copy in small:
         copy.wait()
 
@@ -136,96 +162,89 @@
     live = jnp.sum(jnp.where(routed_here, 1.0, 0.0), axis=0, keepdims=True) > 0.5
     first[1] = jnp.where(live, gate_ref[...] * first[0].astype(F32), 0.0).astype(BF16)
 
-    expected = 1 + (NX - 1) + (NY - 1) + (NZ - 1) + 8
-    pl.semaphore_wait(barrier, expected + jnp.where(home_self, 0, 1) - jnp.where(fin_self, 2, 0))
-
-    links = Links(send_sem, recv_sem, to_z(1))
-    put, take = links.put, links.take
-
-    put(("home", 0), inc_hbm, cols.at[0, home_z, y], relay)
-
     low = pl.ds(0, CUT)
     high = pl.ds(CUT, COLS - CUT)
 
     def gather_steps(a):
         buf = cols.at[a]
-
-        def piece(j, o=0):
-            return buf.at[at_z(j), at_y(o), high]
-
-        def block(j, o):
-            return buf.at[at_z(j), at_y(o), low]
+        mid = CUT + 16 * ((COLS - CUT + 16) // 32)
+        halves = (pl.ds(CUT, mid - CUT), pl.ds(mid, COLS - mid))
+
+        def piece(j, o=0, rows=high):
+            return buf.at[at_z(j), at_y(o), rows]
+
+        def send_z(name, j, d, o, rows):
+            put((name, a, (j - d) % NZ, o, rows.start), piece(j, o, rows), piece(j, o, rows), to_z(d))
+
+        def take_z(name, j, o, rows):
+            take((name, a, j % NZ, o, rows.start), piece(j, o, rows))
 
         def spread(j):
-            put(("y", a, 3, j % NZ), piece(j), piece(j), to_y(1))
-            put(("y", a, 1, j % NZ), piece(j), piece(j), to_y(-1))
-
-        def block_hop(s, o):
-            if s <= 3 or o < 2:
-                put(("bf", a, s, o), block(1 - s, o), block(1 - s, o), to_z(1))
-            if s <= 3 or o >= 2:
-                put(("bb", a, s, o), block(s - 1, o), block(s - 1, o), to_z(-1))
-
-        def forward_up(j):
-            take(("y", a, 3, j % NZ), piece(j, -1))
-            put(("y", a, 2, j % NZ), piece(j, -1), piece(j, -1), to_y(1))
-
-        def forward_down(j):
-            take(("y", a, 1, j % NZ), piece(j, 1))
-            put(("y", a, 2, j % NZ), piece(j, 1), piece(j, 1), to_y(-1))
+            for o in (2, 1, 3):
+                put(("y", a, NY - o, j % NZ), piece(j), piece(j), to_y(o))
+
+        def hop_out(o, rows):
+            for d in (2, -2, 1, -1):
+                send_z("z", 0, d, o, rows)
+
+        def hop_on(o, rows, j):
+            take_z("z", j, o, rows)
+            d = 1 if j < 0 else -1
+            send_z("z", j, d, o, rows)
+            if rows is low:
+                if (j < 0) == (o < 2):
+                    send_z("z", j, 2 * d, o, rows)
+            else:
+                send_z("z", j, 2 * d, o, halves[0] if j < 0 else halves[1])
 
         def start():
             take(("home", a), buf.at[z, y])
+            hop_out(0, high)
+            for o in (2, 1, 3):
+                put(("ly", a, NY - o), piece(0, 0, low), piece(0, 0, low), to_y(o))
+            hop_out(0, low)
+            spread(0)
+
+        def first_hop():
+            hop_on(0, high, -2)
+            hop_on(0, high, 2)
             for o in (1, 3, 2):
-                put(("ly", a, NY - o), block(0, 0), block(0, 0), to_y(o))
-            put(("f", a, 1), piece(0), piece(0), to_z(1))
-            put(("b", a, 1), piece(0), piece(0), to_z(-1))
-            block_hop(1, 0)
-            spread(0)
-
-        def middle(s):
-            take(("f", a, s), piece(-s))
-            if s < 4:
-                put(("f", a, s + 1), piece(-s), piece(-s), to_z(1))
-            if s <= 3:
-                take(("b", a, s), piece(s))
-                if s < 3:
-                    put(("b", a, s + 1), piece(s), piece(s), to_z(-1))
+                take(("ly", a, o), piece(0, o, low))
+                hop_out(o, low)
+            spread(-2)
+            spread(2)
+            for j in (-1, 1):
+                take_z("z", j, 0, high)
+                spread(j)
+            hop_on(0, low, -2)
+            hop_on(0, low, 2)
+
+        def second_hop():
+            for j in (-3, 3):
+                take_z("z", j, 0, high)
+                spread(j)
+            for rows in halves:
+                take_z("z", 4, 0, rows)
+            spread(4)
+            for o in (1, 3, 2):
+                hop_on(o, low, -2)
+                hop_on(o, low, 2)
+
+        def close():
             for o in (0, 1, 3, 2):
-                if s == 1:
-                    if o:
-                        take(("ly", a, o), block(0, o))
-                        block_hop(1, o)
-                else:
-                    take(("bf", a, s - 1, o), block(1 - s, o))
-                    take(("bb", a, s - 1, o), block(s - 1, o))
-                    block_hop(s, o)
-            spread(-s)
-            if s <= 3:
-                spread(s)
-            if s >= 2:
-                forward_up(1 - s)
-            forward_down(s - 1)
-
-        def close():
-            forward_up(-4)
-            for o in range(NY):
-                take(("bf" if o < 2 else "bb", a, 4, o), block(4, o))
-
-        def drain():
-            for j in (0, -1, 1, -2, 2, -3, 3, -4):
-                if j >= 0:
-                    take(("y", a, 3, j % NZ), piece(j, -1))
-                else:
-                    take(("y", a, 1, j % NZ), piece(j, 1))
-                take(("y", a, 2, j % NZ), piece(j, 2))
+                for j in (-1, 1, -3, 3, 4):
+                    take_z("z", j, o, low)
+            for j in (0, -2, 2, -1, 1, -3, 3, 4):
+                for o in (1, 3, 2):
+                    take(("y", a, o, j % NZ), piece(j, o))
                 flatten(a, at_z(j))
 
-        return [start] + [functools.partial(middle, s) for s in range(1, 5)] + [close, drain]
+        return [start, first_hop, second_hop, close]
 
     def flatten(a, slot):
         turned = flip(cols[a, slot].reshape(NY * COLS, TOK)).astype(BF16)
-        flat[lax.rem(slot, 2), pl.ds(pl.multiple_of(lax.div(slot, 2) * TOK, TOK), TOK), :] = turned
+        g, k = slot_holds(x, slot)
+        flat[k, pl.ds(pl.multiple_of(g * TOK, TOK), TOK), :] = turned
 
     def project(i):
         for t in range(2):
@@ -280,23 +299,20 @@
     routed_steps[0]()
     put(("home", 1), first.at[1], cols.at[1, home_z, y], home, home_self)
     routed_steps[1]()
+    scaled_steps[0]()
     routed_steps[2]()
-    for k in range(3, 6):
-        scaled_steps[k - 3]()
-        routed_steps[k]()
+    scaled_steps[1]()
     for copy in w_copies:
         copy.wait()
-    routed_steps[6]()
+    routed_steps[3]()
     project(0)
     part_out(0)
-    scaled_steps[3]()
     project(1)
     part_out(1)
-    scaled_steps[4]()
+    scaled_steps[2]()
     part_on(0)
-    scaled_steps[5]()
     part_on(1)
-    scaled_steps[6]()
+    scaled_steps[3]()
     project(2)
     part_out(2)
 
@@ -313,7 +329,6 @@
     rows_out(0)
     d_all[x, 1] = (d_act * own[1]).astype(BF16)
     rows_out(1)
-    rows_out(2)
 
     nt = (((1,), (1,)), ((), ()))
 
@@ -323,14 +338,33 @@
             out = lax.dot_general(w[0, rows], d_all[g, 0], nt, preferred_element_type=F32)
             out = out + lax.dot_general(w[1, rows], d_all[g, 1], nt, preferred_element_type=F32)
             share[n, k] = out.astype(BF16).reshape(NY, COLS, TOK)
-        for o in (2, 1, 3):
-            put(("sy", n, NY - o), share.at[n, :, at_y(o)], yin.at[n, NY - o - 1], to_y(o))
+        if n == 3:
+            for o in (2, 1, 3):
+                put(("sy", n, NY - o), share.at[n, :, at_y(o)], yin.at[n, NY - o - 1], to_y(o))
+        else:
+            put(("sv", n, 3), share.at[n, 0, at_y(2)], yin.at[n, 1, 0], to_y(1))
+            put(("sv", n, 1), share.at[n, 1, at_y(2)], yin.at[n, 1, 1], to_y(-1))
+            put(("sy", n, 3, 1), share.at[n, 1, at_y(1)], yin.at[n, 2, 1], to_y(1))
+            put(("sy", n, 1, 0), share.at[n, 0, at_y(-1)], yin.at[n, 0, 0], to_y(-1))
+
+    def share_on(n):
+        for k, o in ((0, 1), (1, -1)):
+            take(("sv", n, 2 + o if k == 0 else 1), yin.at[n, 1, k])
+            out = share[n, k, at_y(o)].astype(F32) + yin[n, 1, k].astype(F32)
+            share[n, k, at_y(o)] = out.astype(BF16)
+            put(("sy", n, 3 if o == 1 else 1, k), share.at[n, k, at_y(o)], yin.at[n, 2 if o == 1 else 0, k], to_y(o))
 
     def reduce_y(n):
         out = share[n, :, y].astype(F32)
-        for o in range(1, NY):
-            take(("sy", n, o), yin.at[n, o - 1])
-            out = out + yin[n, o - 1].astype(F32)
+        if n == 3:
+            for o in range(1, NY):
+                take(("sy", n, o), yin.at[n, o - 1])
+                out = out + yin[n, o - 1].astype(F32)
+        else:
+            for o in (1, 3):
+                take(("sy", n, o, 0), yin.at[n, o - 1, 0])
+                take(("sy", n, o, 1), yin.at[n, o - 1, 1])
+                out = out + yin[n, o - 1].astype(F32)
         ysum[n] = out.astype(BF16).reshape(NZ, CHUNK, TOK)
         for o in (4, 3, 5, 2, 6, 1, 7):
             put(("sz", n, NZ - o), ysum.at[n, at_z(o)], zin.at[n, NZ - o - 1], to_z(o))
@@ -346,11 +380,11 @@
 
     def weight_grad(i):
         a = 0 if i < 2 else 1
-        right = d_all[:, i].reshape(NX * TOK, HID)
+        right = jnp.concatenate([d_all[at_x(m), i] for m in range(NX)], axis=0)
         for k in range(2):
             for q in range(2):
                 left = jnp.concatenate(
-                    [cols[a, 2 * g + k, pl.ds(2 * q, 2)].reshape(384, TOK) for g in range(NX)], axis=1)
+                    [cols[a, slot_of(x, m, k), pl.ds(2 * q, 2)].reshape(384, TOK) for m in range(NX)], axis=1)
                 out = jnp.dot(left, right, preferred_element_type=F32)
                 wg[0, i, 768 * k + 384 * q:768 * k + 384 * q + 384] = out.astype(BF16)
 
@@ -358,19 +392,23 @@
     make_share(0, x)
     rows_on(0)
     rows_on(1)
+    rows_out(2)
+    share_on(0)
     make_share(1, at_x(1))
+    make_share(2, at_x(-1))
     reduce_y(0)
-    make_share(2, at_x(-1))
-    reduce_y(1)
-    reduce_z(0, order[0])
-    rows_on(2)
+    share_on(1)
+    share_on(2)
     rows_far(0)
     rows_far(1)
     make_share(3, at_x(2))
+    rows_on(2)
+    reduce_y(1)
     reduce_y(2)
-    reduce_z(1, order[1])
+    reduce_z(0, order[0])
     weight_grad(0)
     reduce_y(3)
+    reduce_z(1, order[1])
     reduce_z(2, order[2])
     weight_grad(1)
     reduce_z(3, order[3])

time: 97.3 us -> 93.3 us (0.959)
  Pallas kernels: 93 us -> 89.2 us
    pallas_call x1, Pallas kernels: 93 us -> 89.2 us  [on_device(): pl.pallas_call(kernel, out_shape=(jax.ShapeDtypeStruct((COLS, TOK), BF16)...]
where the time goes in v3:
time: 93.3 us; the launch traced here: 93.2 us
  Pallas kernels  89.2 us (96%)
  local copies, waits for them, and re-layouts  2.81 us (3%)
  between operations  1.29 us (1%)
    pallas_call x1, Pallas kernels, on_device(): pl.pallas_call(kernel, out_shape=(jax.ShapeDtypeStruct((COLS, TOK), BF16)...  89.2 us
    unnamed x2, local copies, waits for them, and re-layouts  2.81 us

profile of v3, /device:TPU:36, one launch (start us, length us, event | category | flops | bytes accessed | tf_op | source)
XLA Modules:
  0.0 93.2 jit_solution(5191056661496701989)
XLA Ops:
  1.3 89.2 %expert.1 = (bf16[192,128]{1,0:T(8,128)(2,1)S(1)}, bf16[1,3,1536,512]{3,2,1,0:T(8,128)(2,1)S(1)}) custom-call(bf16[192,128]{1,0:T(8,128)(2,1)} %bitcast.8, bf16[192,128]{1,0:T(8,128)(2,1)} %bitcast.9, bf16[1,3,1536,512]{3,2,1,0:T(8,128)(2,1)} %w_hbm.1, s32[1,128]{1,0:T(1,128)} %bitcast.10, s32[1,1]{1,0:T(1,128)} %bitcast.6.count_ref, f32[1,128]{1,0:T(1,128)} %bitcast.11), custom_call_target="tpu_custom_call" | custom-call | flops 6400000000 | bytes 10000000 | tf_op jit(solution)/shard_map/expert/pallas_call | solution.py:430
  90.4 0.6 copy.11
  91.1 2.2 %copy.12 = bf16[1,3,1536,512]{3,2,1,0:T(8,128)(2,1)} copy(bf16[1,3,1536,512]{3,2,1,0:T(8,128)(2,1)S(1)} %get-tuple-element.9) | data formatting | bytes 9437184

commit v4 on v3

--- a/solution.py
+++ b/solution.py
@@ -12,7 +12,7 @@
 COLS = 192
 ROWS_D = 1536
 HID = 512
-CUT = 80
+CUT = 64
 CHUNK = 48
 F32 = jnp.float32
 BF16 = jnp.bfloat16
@@ -231,10 +231,10 @@
                 hop_on(o, low, 2)
 
         def close():
-            for o in (0, 1, 3, 2):
-                for j in (-1, 1, -3, 3, 4):
-                    take_z("z", j, o, low)
             for j in (0, -2, 2, -1, 1, -3, 3, 4):
+                if j in (-1, 1, -3, 3, 4):
+                    for o in (0, 1, 3, 2):
+                        take_z("z", j, o, low)
                 for o in (1, 3, 2):
                     take(("y", a, o, j % NZ), piece(j, o))
                 flatten(a, at_z(j))
@@ -278,22 +278,25 @@
         take(("part", i, 1, 1), xin.at[1, i, lower])
         return part[x, i].astype(F32) + xin[0, i].astype(F32) + xin[1, i].astype(F32)
 
-    def rows_out(i):
-        mine = d_all.at[x, i]
-        put(("row", i, 3), mine, mine, to_x(1))
-        put(("row", i, 1), mine, mine, to_x(-1))
-
-    def rows_on(i):
-        take(("row", i, 3), d_all.at[at_x(-1), i])
-        onward = d_all.at[at_x(-1), i, upper]
-        put(("far", i, 0), onward, onward, to_x(1))
-        take(("row", i, 1), d_all.at[at_x(1), i])
-        onward = d_all.at[at_x(1), i, lower]
-        put(("far", i, 1), onward, onward, to_x(-1))
-
-    def rows_far(i):
-        take(("far", i, 0), d_all.at[at_x(2), i, upper])
-        take(("far", i, 1), d_all.at[at_x(2), i, lower])
+    def rows_of(o, lo, n, rows):
+        return d_all.at[at_x(o), pl.ds(lo, n), rows]
+
+    def rows_out(lo, n):
+        for first_half in (True, False):
+            for o in (1, -1):
+                rows = upper if (o == 1) == first_half else lower
+                put(("row", lo, NX - 1 if o == 1 else 1, first_half), rows_of(0, lo, n, rows), rows_of(0, lo, n, rows), to_x(o))
+
+    def rows_on(lo, n):
+        for o, rows in ((-1, upper), (1, lower)):
+            take(("row", lo, o % NX, True), rows_of(o, lo, n, rows))
+            put(("far", lo, o), rows_of(o, lo, n, rows), rows_of(o, lo, n, rows), to_x(-o))
+        for o, rows in ((-1, lower), (1, upper)):
+            take(("row", lo, o % NX, False), rows_of(o, lo, n, rows))
+
+    def rows_far(lo, n):
+        for o, rows in ((-1, upper), (1, lower)):
+            take(("far", lo, o), rows_of(2, lo, n, rows))
 
     routed_steps, scaled_steps = gather_steps(0), gather_steps(1)
     routed_steps[0]()
@@ -326,9 +329,8 @@
     part_on(2)
     d_act = total(2)
     d_all[x, 0] = (d_act * own[0]).astype(BF16)
-    rows_out(0)
     d_all[x, 1] = (d_act * own[1]).astype(BF16)
-    rows_out(1)
+    rows_out(0, 2)
 
     nt = (((1,), (1,)), ((), ()))
 
@@ -390,19 +392,17 @@
 
     order = (0, 1, 3, 2)
     make_share(0, x)
-    rows_on(0)
-    rows_on(1)
-    rows_out(2)
+    rows_on(0, 2)
+    rows_out(2, 1)
     share_on(0)
     make_share(1, at_x(1))
     make_share(2, at_x(-1))
     reduce_y(0)
     share_on(1)
     share_on(2)
-    rows_far(0)
-    rows_far(1)
+    rows_far(0, 2)
     make_share(3, at_x(2))
-    rows_on(2)
+    rows_on(2, 1)
     reduce_y(1)
     reduce_y(2)
     reduce_z(0, order[0])
@@ -412,7 +412,7 @@
     reduce_z(2, order[2])
     weight_grad(1)
     reduce_z(3, order[3])
-    rows_far(2)
+    rows_far(2, 1)
     weight_grad(2)
     take(("end",), fin)
     din_ref[...] = fin[...].reshape(COLS, TOK)

time: 93.3 us -> 93.1 us (level)
  no operation moved by 1% of the time
where the time goes in v4:
time: 93.1 us; the launch traced here: 93 us
  Pallas kernels  88.9 us (95%)
  local copies, waits for them, and re-layouts  2.81 us (3%)
  between operations  1.29 us (1%)
    pallas_call x1, Pallas kernels, on_device(): pl.pallas_call(kernel, out_shape=(jax.ShapeDtypeStruct((COLS, TOK), BF16)...  88.9 us
    unnamed x2, local copies, waits for them, and re-layouts  2.81 us

profile of v4, /device:TPU:36, one launch (start us, length us, event | category | flops | bytes accessed | tf_op | source)
XLA Modules:
  0.0 93.0 jit_solution(5574702462218511835)
XLA Ops:
  1.3 88.9 %expert.1 = (bf16[192,128]{1,0:T(8,128)(2,1)S(1)}, bf16[1,3,1536,512]{3,2,1,0:T(8,128)(2,1)S(1)}) custom-call(bf16[192,128]{1,0:T(8,128)(2,1)} %bitcast.8, bf16[192,128]{1,0:T(8,128)(2,1)} %bitcast.9, bf16[1,3,1536,512]{3,2,1,0:T(8,128)(2,1)} %w_hbm.1, s32[1,128]{1,0:T(1,128)} %bitcast.10, s32[1,1]{1,0:T(1,128)} %bitcast.6.count_ref, f32[1,128]{1,0:T(1,128)} %bitcast.11), custom_call_target="tpu_custom_call" | custom-call | flops 6400000000 | bytes 10000000 | tf_op jit(solution)/shard_map/expert/pallas_call | solution.py:430
  90.2 0.6 copy.11
  90.8 2.2 %copy.12 = bf16[1,3,1536,512]{3,2,1,0:T(8,128)(2,1)} copy(bf16[1,3,1536,512]{3,2,1,0:T(8,128)(2,1)S(1)} %get-tuple-element.9) | data formatting | bytes 9437184
